TPU v7x, 32 devices: a whole 2x2x4 slice. The times are simulated.
32 devices in a mesh: grp: 2 (over y), kvp: 4 (over z), tp: 4 (over x, core).
Axes of the slice: x: 2, y: 2, z: 4, core: 2. Of those that a mesh axis runs over, the one named last changes fastest.
Arguments:
- queries: bfloat16 [32, 4096], P('grp', 'tp'), parts along dimension 0, may hold values from -6 to 6
- keys: bfloat16 [32, 512, 512], P('grp', 'kvp', 'tp'), parts along dimension 0, may hold values from -6 to 6
- values: bfloat16 [32, 512, 512], P('grp', 'kvp', 'tp'), parts along dimension 0, may hold values from -6 to 6
- lengths: int32 [32], P('grp'), parts along dimension 0, may hold values from 256 to 512, as said below
- out_weight: bfloat16 [4096, 1536], P('tp', 'kvp'), may hold values from -0.375 to 0.375
- residual: bfloat16 [32, 1536], P('grp', 'kvp'), parts along dimension 0, may hold values from -20 to 20
- norm_gain: bfloat16 [1536], P('kvp'), may hold values from 0.099609375 to 1.8984375
- expert_ids: int32 [32, 4], P('grp'), parts along dimension 0, may hold values from 0 to 3, as said below
- gate_probs: float32 [32, 4], P('grp'), parts along dimension 0, may hold values from 0.2 to 1
- w_gate: bfloat16 [4, 1536, 1536], P('kvp', None, 'tp'), may hold values from -0.15625 to 0.15625
- w_up: bfloat16 [4, 1536, 1536], P('kvp', None, 'tp'), may hold values from -0.15625 to 0.15625
- w_down: bfloat16 [4, 1536, 1536], P('kvp', 'tp'), may hold values from -0.15625 to 0.15625
Outputs:
- attended: float32 [32, 4096], P('grp', 'tp'), parts along dimension 0
- mixed: bfloat16 [32, 1536], P('grp', 'kvp'), parts along dimension 0
There are 2 independent parts, one for each index of `grp`. A program takes and returns all parts, laid end to end along the dimension named above; an argument that names none is the same for every part. Nothing has to cross between parts.
Inputs may be any that keep to these rules, and one draw needn't show every extreme that they name: `lengths`: at least one sequence has all 512 positions valid. `expert_ids`: each row names 4 different experts; no expert is named by more than 16 rows, and some expert by exactly 16.
All inputs are finite; a program needn't handle non-finite values.
Results may differ from a plain program's by a relative error of at most 0.006.
Values may be sent and summed in bfloat16 or wider, within the bound.
A program may use at most 64 MiB of HBM per device.

v0:
```python
import jax
import jax.numpy as jnp
from jax import lax
from jax.sharding import PartitionSpec as P

D = 1536
HEAD = 64


EPSILON = 1e-05
NEGATIVE = -1e30


def merged(part, axis, combine):
    gathered = jax.tree.map(lambda a: lax.all_gather(a, axis), part)

    def take(source):
        return jax.tree.map(lambda a: lax.dynamic_index_in_dim(a, source, 0, False), gathered)

    return lax.fori_loop(
        1, lax.axis_size(axis), lambda source, state: combine(state, take(source)), take(0)
    )


def slot_tables(expert_ids, gate_probs, experts, capacity):
    batch_size, top_count = expert_ids.shape
    flat_ids = expert_ids.reshape(-1)
    pair_count = flat_ids.shape[0]
    pair_order = jnp.arange(pair_count, dtype=jnp.int32)
    earlier_same = (flat_ids[:, None] == flat_ids[None, :]) & (
        pair_order[None, :] < pair_order[:, None]
    )
    slot_index = jnp.sum(earlier_same.astype(jnp.int32), axis=1)
    target_col = flat_ids * capacity + slot_index
    columns = jnp.arange(experts * capacity, dtype=jnp.int32)
    hit_table = (target_col[:, None] == columns[None, :]).astype(jnp.float32)
    hit_table = hit_table.reshape(batch_size, top_count, experts * capacity)
    dispatch = jnp.sum(hit_table, axis=1)
    combine = jnp.sum(hit_table * gate_probs[:, :, None], axis=1)
    return (dispatch, combine)


def merge_partial(earlier, latest):
    global_max = jnp.maximum(earlier[0], latest[0])
    lead_scale = jnp.exp(earlier[0] - global_max)
    trail_scale = jnp.exp(latest[0] - global_max)
    return (
        global_max,
        lead_scale * earlier[1] + trail_scale * latest[1],
        lead_scale[..., None] * earlier[2] + trail_scale[..., None] * latest[2],
    )


def on_device(
    queries,
    keys,
    values,
    lengths,
    out_weight,
    residual,
    norm_gain,
    expert_ids,
    gate_probs,
    w_gate,
    w_up,
    w_down,
):
    batch_size = queries.shape[0]
    local_kv = keys.shape[2] // HEAD
    local_heads = queries.shape[1] // HEAD
    group_size = local_heads // local_kv
    ctx_dev = keys.shape[1]
    shards = lax.axis_size("kvp")
    query_heads = queries.reshape(batch_size, local_kv, group_size, HEAD)
    key_rows = keys.reshape(batch_size, ctx_dev, local_kv, HEAD)
    value_rows = values.reshape(batch_size, ctx_dev, local_kv, HEAD)
    scores = jnp.einsum(
        "bgrd,bcgd->bgrc", query_heads, key_rows, preferred_element_type=jnp.float32
    ) * HEAD ** (-0.5)
    position = lax.axis_index("kvp") * ctx_dev + jnp.arange(ctx_dev, dtype=jnp.int32)
    valid_key = (position[None, :] < lengths[:, None])[:, None, None, :]
    masked = jnp.where(valid_key, scores, NEGATIVE)
    block_max = jnp.max(masked, axis=3)
    weights = jnp.where(valid_key, jnp.exp(masked - block_max[..., None]), 0.0)
    rounded = weights.astype(jnp.bfloat16)
    block_sum = jnp.sum(rounded.astype(jnp.float32), axis=3)
    block_out = jnp.einsum(
        "bgrc,bcgd->bgrd", rounded, value_rows, preferred_element_type=jnp.float32
    )
    global_max, denominator, summed = merged(
        (block_max, block_sum, block_out), "kvp", merge_partial
    )
    attended = (summed / denominator[..., None]).reshape(batch_size, local_heads * HEAD)
    projected = lax.psum(
        jnp.dot(attended.astype(jnp.bfloat16), out_weight, preferred_element_type=jnp.float32), "tp"
    )
    hidden_state = lax.optimization_barrier(
        (projected + residual.astype(jnp.float32)).astype(jnp.bfloat16)
    )
    state_wide = hidden_state.astype(jnp.float32)
    col_count = hidden_state.shape[1]
    exp_dev = w_gate.shape[0]
    experts = exp_dev * shards
    capacity = min(batch_size, max(2, 2 * batch_size * expert_ids.shape[1] // experts))
    dispatch, combine = slot_tables(expert_ids, gate_probs, experts, capacity)
    total_sq = lax.psum(jnp.sum(state_wide * state_wide, axis=1), "kvp")
    inverse = lax.rsqrt(total_sq / D + EPSILON)
    normed = (state_wide * inverse[:, None] * norm_gain.astype(jnp.float32)[None, :]).astype(
        jnp.bfloat16
    )
    outgoing = jnp.dot(
        dispatch.T.astype(jnp.bfloat16), normed, preferred_element_type=jnp.float32
    ).astype(jnp.bfloat16)
    outgoing = outgoing.reshape(experts, capacity, col_count)
    expert_rows = lax.all_to_all(outgoing, "kvp", split_axis=0, concat_axis=2, tiled=True)
    gate_proj = jnp.einsum("ecd,edf->ecf", expert_rows, w_gate, preferred_element_type=jnp.float32)
    up_proj = jnp.einsum("ecd,edf->ecf", expert_rows, w_up, preferred_element_type=jnp.float32)
    activation = (jax.nn.silu(gate_proj) * up_proj).astype(jnp.bfloat16)
    partial_value = jnp.einsum(
        "ecf,efd->ecd", activation, w_down, preferred_element_type=jnp.float32
    )
    returned = lax.all_to_all(partial_value, "kvp", split_axis=2, concat_axis=0, tiled=True)
    moe_local = jnp.dot(
        combine, returned.reshape(experts * capacity, col_count), precision=lax.Precision.HIGHEST
    )
    moe_term = lax.psum(moe_local, "tp")
    mixed = (state_wide + moe_term).astype(jnp.bfloat16)
    return (attended, mixed)


def solution(mesh):
    return jax.shard_map(
        on_device,
        mesh=mesh,
        in_specs=(
            P("grp", "tp"),
            P("grp", "kvp", "tp"),
            P("grp", "kvp", "tp"),
            P("grp"),
            P("tp", "kvp"),
            P("grp", "kvp"),
            P("kvp"),
            P("grp", None),
            P("grp", None),
            P("kvp", None, "tp"),
            P("kvp", None, "tp"),
            P("kvp", "tp", None),
        ),
        out_specs=(P("grp", "tp"), P("grp", "kvp")),
        check_vma=False,
    )
```

profile of v0, /device:TPU:0, one launch (start us, length us, event | category | flops | bytes accessed | tf_op | source)
XLA Modules:
  0.0 124.9 jit_solution(10427162739778779653)
XLA Ops:
  0.7 0.8 convert_element_type.54
  1.4 0.8 copy.99
  2.2 0.1 eq.13
  2.3 0.2 convert_reduce_fusion.2
  2.5 0.1 reduce_sum.49
  2.6 0.1 copy.100
  2.6 1.3 %multiply_add_fusion = s32[16,4]{0,1:T(4,128)} fusion(s32[16,4]{0,1:T(4,128)S(1)} %copy.100, s32[16,4]{0,1:T(4,128)} %param.21), kind=kLoop, calls=%fused_computation.48 | loop fusion | flops 128 | bytes 768 | tf_op jit(solution)/shard_map/add | solution.py:34
  3.9 0.9 reshape.104
  4.8 1.4 %copy.90 = bf16[16,128,128]{1,2,0:T(8,128)(2,1)S(1)} copy(bf16[16,128,128]{2,1,0:T(8,128)(2,1)} %param.15) | data formatting | bytes 1048576 | tf_op args[1]
  6.3 0.3 fusion.39
  6.6 14.9 %all-gather = f32[64,2,8]{2,1,0:T(2,128)S(1)} all-gather(f32[16,2,8]{2,1,0:T(2,128)S(1)} %get-tuple-element.236), channel_id=2, replica_groups=mesh['grp'=2,'kvp'=4,'tp'=4] {'kvp'}, dimensions={0}, use_global_device_ids=true | all-gather | bytes 5120 | tf_op jit(solution)/shard_map/all_gather | solution.py:15
  21.5 0.2 convert_reduce_fusion
  21.7 13.3 %all-gather.1 = f32[64,2,8]{2,1,0:T(2,128)S(1)} all-gather(f32[16,2,8]{2,1,0:T(2,128)S(1)} %convert_reduce_fusion), channel_id=3, replica_groups=mesh['grp'=2,'kvp'=4,'tp'=4] {'kvp'}, dimensions={0}, use_global_device_ids=true | all-gather | bytes 5120 | tf_op jit(solution)/shard_map/all_gather | solution.py:15
  35.1 0.1 copy.97
  35.3 0.1 copy.96
  35.4 0.3 copy.91
  35.7 0.4 fusion.35
  36.1 15.2 %all-gather.2 = f32[64,2,8,64]{3,2,1,0:T(8,128)S(1)} all-gather(f32[16,2,8,64]{3,2,1,0:T(8,128)S(1)} %fusion.35), channel_id=4, replica_groups=mesh['grp'=2,'kvp'=4,'tp'=4] {'kvp'}, dimensions={0}, use_global_device_ids=true | all-gather | bytes 327680 | tf_op jit(solution)/shard_map/all_gather | solution.py:15
  51.3 1.1 while.19
  51.3 0.1 copy.113
  51.5 0.2 fusion.53
  51.7 0.1 copy.113
  51.9 0.2 fusion.53
  52.2 0.2 fusion.53
  52.5 0.1 broadcast_divide_fusion
  52.6 0.7 reshape.107
  53.4 2.1 %fusion.18 = f32[16,384]{1,0:T(8,128)} fusion(bf16[1024,384]{1,0:T(8,128)(2,1)} %param.18, f32[16,1024]{1,0:T(8,128)} %reshape.107), kind=kOutput, calls=%fused_computation.30 | convolution fusion | flops 12599296 | bytes 876544 | tf_op jit(solution)/shard_map/dot_general | solution.py:95
  55.4 11.4 %psum.21 = f32[16,384]{1,0:T(8,128)} all-reduce(f32[16,384]{1,0:T(8,128)} %fusion.18), channel_id=1, replica_groups=mesh['grp'=2,'kvp'=4,'tp'=4] {'tp'}, use_global_device_ids=true, to_apply=%region_4.5 | all-reduce | flops 6144 | bytes 49152 | tf_op jit(solution)/shard_map/psum | solution.py:94
  66.8 0.7 add_convert_fusion
  67.5 0.6 fusion.21
  68.2 12.5 %psum.22 = f32[16]{0:T(128)} all-reduce(f32[16]{0:T(128)} %fusion.21), channel_id=1, replica_groups=mesh['grp'=2,'kvp'=4,'tp'=4] {'kvp'}, use_global_device_ids=true, to_apply=%region_9.10 | all-reduce | flops 16 | bytes 128 | tf_op jit(solution)/shard_map/psum | solution.py:106
  80.7 0.7 add_rsqrt_fusion
  81.3 1.4 %convert_reduce_fusion.1 = (bf16[16,64]{1,0:T(8,128)(2,1)S(1)}, f32[16,64]{1,0:T(8,128)}) fusion(s32[16,4]{0,1:T(4,128)} %multiply_add_fusion, f32[16,4]{0,1:T(4,128)} %param.22), kind=kLoop, calls=%fused_computation.25 | loop fusion | flops 18432 | bytes 6656 | tf_op jit(solution)/shard_map/reduce_sum | solution.py:38
  82.7 0.2 convolution_convert_fusion
  82.9 8.1 %all_to_all.30 = bf16[4,16,384]{2,1,0:T(8,128)(2,1)S(1)} all-to-all(bf16[4,16,384]{2,1,0:T(8,128)(2,1)S(1)} %bitcast.73), channel_id=1, replica_groups=mesh['grp'=2,'kvp'=4,'tp'=4] {'kvp'}, dimensions={0} | all-to-all | bytes 98304 | tf_op jit(solution)/shard_map/all_to_all | solution.py:115
  91.0 0.6 copy.110
  91.6 1.7 %fusion.7 = f32[16,384]{1,0:T(8,128)} fusion(bf16[16,1536]{1,0:T(8,128)(2,1)} %bitcast.23, bf16[1,1536,384]{2,1,0:T(8,128)(2,1)S(1)} %copy-done.2), kind=kOutput, calls=%fused_computation.12 | convolution fusion | flops 18874368 | bytes 1253376 | tf_op jit(solution)/shard_map/ecd,edf->ecf/dot_general | solution.py:116
  93.3 1.6 %fusion.3 = f32[16,1536]{0,1:T(8,128)S(1)} fusion(bf16[1,384,1536]{2,1,0:T(8,128)(2,1)S(1)} %copy-done, bf16[16,1536]{1,0:T(8,128)(2,1)} %bitcast.23, bf16[1,1536,384]{2,1,0:T(8,128)(2,1)S(1)} %copy-done.1, f32[16,384]{1,0:T(8,128)} %fusion.7), kind=kOutput, calls=%fused_computation.8 | convolution fusion | flops 37785600 | bytes 2531328 | tf_op jit(solution)/shard_map/ecf,efd->ecd/dot_general | solution.py:119
  95.0 0.6 broadcast.55
  95.5 7.2 %reduce = f32[1536,16]{1,0:T(8,128)S(1)} reduce(f32[1536,1,16]{2,1,0:T(1,128)S(1)} %bitcast.66, f32[]{:T(128)} %broadcast.55), dimensions={1}, to_apply=%bitcast.47.reduce_sub_computation | reduce | bytes 196612
  102.8 0.3 reshape.123
  103.1 8.2 %all_to_all.31 = f32[4,1,6144]{2,1,0:T(1,128)S(1)} all-to-all(f32[4,1,6144]{2,1,0:T(1,128)S(1)} %reshape.123), channel_id=1, replica_groups=mesh['grp'=2,'kvp'=4,'tp'=4] {'kvp'}, dimensions={0} | all-to-all | bytes 196608 | tf_op jit(solution)/shard_map/all_to_all | solution.py:122
  111.3 0.9 reduce.1
  112.2 1.3 %reshape.124 = f32[1536,1,16]{2,1,0:T(1,128)S(1)} reshape(f32[4,6144]{1,0:T(4,128)S(1)} %reduce.1) | data formatting | bytes 196608
  113.6 0.2 copy.109
  113.8 0.2 fusion.40
  114.0 10.3 %psum.23 = f32[16,384]{1,0:T(8,128)S(1)} all-reduce(f32[16,384]{1,0:T(8,128)S(1)} %fusion.40), channel_id=1, replica_groups=mesh['grp'=2,'kvp'=4,'tp'=4] {'tp'}, use_global_device_ids=true, to_apply=%region_10.11 | all-reduce | flops 6144 | bytes 49152 | tf_op jit(solution)/shard_map/psum | solution.py:126
  124.3 0.6 fusion.24
  (29 shorter events, 0.8 us)
Async XLA Ops:
  0.6 92.7 %copy-start = (bf16[1,384,1536]{2,1,0:T(8,128)(2,1)S(1)}, bf16[1,384,1536]{2,1,0:T(8,128)(2,1)}, u32[]{:S(2)}) copy-start(bf16[1,384,1536]{2,1,0:T(8,128)(2,1)} %param.25) | copy-start | bytes 3538948
  0.6 5.5 %copy-start.5 = (s32[16]{0:T(128)S(1)}, s32[16]{0:T(128)}, u32[]{:S(2)}) copy-start(s32[16]{0:T(128)} %param.17) | copy-start | bytes 196
  4.8 30.6 %copy-start.3 = (bf16[16,128,128]{2,1,0:T(8,128)(2,1)S(1)}, bf16[16,128,128]{2,1,0:T(8,128)(2,1)}, u32[]{:S(2)}) copy-start(bf16[16,128,128]{2,1,0:T(8,128)(2,1)} %param.16) | copy-start | bytes 1572868
  52.4 39.2 %copy-start.2 = (bf16[1,1536,384]{2,1,0:T(8,128)(2,1)S(1)}, bf16[1,1536,384]{2,1,0:T(8,128)(2,1)}, u32[]{:S(2)}) copy-start(bf16[1,1536,384]{2,1,0:T(8,128)(2,1)} %param.23) | copy-start | bytes 3538948
  53.4 40.0 %copy-start.1 = (bf16[1,1536,384]{2,1,0:T(8,128)(2,1)S(1)}, bf16[1,1536,384]{2,1,0:T(8,128)(2,1)}, u32[]{:S(2)}) copy-start(bf16[1,1536,384]{2,1,0:T(8,128)(2,1)} %param.24) | copy-start | bytes 3538948
  103.1 10.8 %copy-start.4 = (f32[16,64]{1,0:T(8,128)S(1)}, f32[16,64]{1,0:T(8,128)}, u32[]{:S(2)}) copy-start(f32[16,64]{1,0:T(8,128)} %get-tuple-element.217) | copy-start | bytes 12292
where the time goes:
time: 126 us; the launch traced here: 125 us
  blocking collectives  93.8 us (74%)
  other arithmetic  15.3 us (12%)
  local copies, waits for them, and re-layouts  8.31 us (7%)
  matrix products  6.53 us (5%)
    all_gather x3, blocking collectives, merged(): gathered = jax.tree.map(lambda a: lax.all_gather(a, axis), part)  43.4 us
    psum x1, blocking collectives, on_device(): total_sq = lax.psum(jnp.sum(state_wide * state_wide, axis=1), 'kvp')  12.5 us
    psum x1, blocking collectives, on_device(): lax.psum(jnp.dot(attended.astype(jnp.bfloat16), out_weight, preferred_ele...  11.4 us
    psum x1, blocking collectives, on_device(): moe_term = lax.psum(moe_local, 'tp')  10.3 us
    all_to_all x1, blocking collectives, on_device(): lax.all_to_all(partial_value, 'kvp', split_axis=2, concat_axis=0, tiled=T...  8.21 us
    all_to_all x1, blocking collectives, on_device(): lax.all_to_all(outgoing, 'kvp', split_axis=0, concat_axis=2, tiled=True)  8.06 us
    unnamed x1, other arithmetic  7.21 us
    unnamed x19, local copies, waits for them, and re-layouts  5.3 us

commit v1 on v0

--- a/solution.py
+++ b/solution.py
@@ -1,7 +1,11 @@
 import jax
 import jax.numpy as jnp
 from jax import lax
+from jax.experimental import pallas as pl
+from jax.experimental.pallas import tpu as pltpu
 from jax.sharding import PartitionSpec as P
+
+MESH = pl.DeviceIdType.MESH
 
 D = 1536
 HEAD = 64
@@ -128,9 +132,294 @@
     return (attended, mixed)
 
 
+NORM_WIDTH = D
+
+
+def peers(axis):
+    count = lax.axis_size(axis)
+    me = lax.axis_index(axis)
+    return [(step - 1, lax.rem(me + step, count)) for step in range(1, count)]
+
+
+def fused(
+    q_hbm, k_hbm, v_hbm, len_ref, wo_hbm, res_ref, gain_ref, ids_ref, gp_ref, wg_hbm, wu_hbm, wd_hbm,
+    att_ref, mix_ref,
+    q_vm, k_vm, v_vm, wo_vm, wg_vm, wu_vm, wd_vm,
+    q_rows, s_rows, o_rows, t_rows,
+    o_all, stat_all, gain_all, p_all, h_all, y_send, y_recv, z_all,
+    load_sem, o_send, o_recv, st_send, st_recv, g_send, g_recv,
+    p_send, p_recv, h_send, h_recv, ys_send, ys_recv, z_send, z_recv,
+):
+    shards = o_all.shape[0]
+    tps = p_all.shape[0]
+    batch, width = q_vm.shape
+    heads = width // HEAD
+    ctx = k_vm.shape[1]
+    lanes = k_vm.shape[2]
+    cols = wo_vm.shape[1]
+    group = heads * HEAD // lanes
+    mine = lax.axis_index("kvp")
+    my_tp = lax.axis_index("tp")
+    kvp_peers = peers("kvp")
+    tp_peers = peers("tp")
+
+    loads = []
+    for index, (source, target) in enumerate(
+        ((q_hbm, q_vm), (k_hbm, k_vm), (v_hbm, v_vm), (wo_hbm, wo_vm), (wg_hbm, wg_vm), (wu_hbm, wu_vm), (wd_hbm, wd_vm))
+    ):
+        copy = pltpu.make_async_copy(source, target, load_sem.at[index])
+        copy.start()
+        loads.append(copy)
+    q_load, k_load, v_load, wo_load, wg_load, wu_load, wd_load = loads
+
+    barrier = pltpu.get_barrier_semaphore()
+    for _, peer in kvp_peers:
+        pl.semaphore_signal(barrier, inc=1, device_id={"kvp": peer}, device_id_type=MESH)
+    for _, peer in tp_peers:
+        pl.semaphore_signal(barrier, inc=1, device_id={"tp": peer}, device_id_type=MESH)
+
+    sent = []
+
+    def push(source, target, send, recv, place):
+        copy = pltpu.make_async_remote_copy(
+            src_ref=source, dst_ref=target, send_sem=send, recv_sem=recv,
+            device_id=place, device_id_type=MESH,
+        )
+        copy.start()
+        sent.append(copy)
+        return copy
+
+    lane = lax.broadcasted_iota(jnp.int32, (batch, lanes), 1)
+    low = lane < HEAD
+    gain_all[mine] = jnp.broadcast_to(gain_ref[...].astype(jnp.float32).reshape(1, cols), (8, cols))
+
+    q_load.wait()
+    for head in range(heads):
+        pair = head // 2
+        wide = q_vm[:, pair * lanes : (pair + 1) * lanes].astype(jnp.float32)
+        kept = jnp.where(low if head % 2 == 0 else ~low, wide, 0.0)
+        if head % 2 != head // group:
+            kept = pltpu.roll(kept, HEAD, 1)
+        q_rows[pl.ds(head, batch, stride=heads), :] = kept
+
+    k_load.wait()
+    position = mine * ctx + lax.broadcasted_iota(jnp.int32, (heads, ctx), 1)
+    for b in range(batch):
+        rows = pl.ds(b * heads, heads)
+        scores = lax.dot_general(
+            q_rows[rows, :].astype(jnp.bfloat16), k_vm[b],
+            (((1,), (1,)), ((), ())), preferred_element_type=jnp.float32,
+        ) * HEAD ** (-0.5)
+        s_rows[rows, :] = jnp.where(position < len_ref[b], scores, NEGATIVE)
+    v_load.wait()
+    stat_low = lax.broadcasted_iota(jnp.int32, (heads, lanes), 1) < HEAD
+    for b in range(batch):
+        rows = pl.ds(b * heads, heads)
+        masked = s_rows[rows, :]
+        block_max = jnp.max(masked, axis=1, keepdims=True)
+        weights = jnp.where(position < len_ref[b], jnp.exp(masked - block_max), 0.0)
+        rounded = weights.astype(jnp.bfloat16)
+        block_sum = jnp.sum(rounded.astype(jnp.float32), axis=1, keepdims=True)
+        out = jnp.dot(rounded, v_vm[b], preferred_element_type=jnp.float32)
+        o_rows[pl.ds(b, heads, stride=batch), :] = out
+        t_rows[pl.ds(b, heads, stride=batch), :] = jnp.where(stat_low, block_max, block_sum)
+    stat = jnp.ones((batch, lanes), jnp.float32)
+    for pair in range(heads // 2):
+        first = o_rows[2 * pair * batch : (2 * pair + 1) * batch, :]
+        second = o_rows[(2 * pair + 1) * batch : (2 * pair + 2) * batch, :]
+        if 2 * pair // group == 0:
+            second = pltpu.roll(second, HEAD, 1)
+        else:
+            first = pltpu.roll(first, HEAD, 1)
+        o_all[mine, :, pair * lanes : (pair + 1) * lanes] = jnp.where(low, first, second).astype(jnp.bfloat16)
+    for head in range(heads):
+        stat = jnp.where((lane == head) | (lane == HEAD + head), t_rows[head * batch : (head + 1) * batch, :], stat)
+    stat_all[mine] = stat
+
+    pl.semaphore_wait(barrier, len(kvp_peers) + len(tp_peers))
+    o_copies = []
+    for slot, peer in kvp_peers:
+        o_copies.append(push(stat_all.at[mine], stat_all.at[mine], st_send.at[slot], st_recv.at[slot], {"kvp": peer}))
+        o_copies.append(push(o_all.at[mine], o_all.at[mine], o_send.at[slot], o_recv.at[slot], {"kvp": peer}))
+    g_copies = [
+        push(gain_all.at[mine], gain_all.at[mine], g_send.at[slot], g_recv.at[slot], {"kvp": peer})
+        for slot, peer in kvp_peers
+    ]
+    wo_load.wait()
+    for copy in o_copies:
+        copy.wait_recv()
+
+    global_max = stat_all[0]
+    for s in range(1, shards):
+        global_max = jnp.maximum(global_max, stat_all[s])
+    scales = []
+    denominator = None
+    for s in range(shards):
+        stat = stat_all[s]
+        scale = jnp.exp(stat - global_max)
+        scales.append(scale)
+        term = scale * pltpu.roll(stat, HEAD, 1)
+        denominator = term if denominator is None else denominator + term
+    inverse = 1.0 / denominator
+    factors = [scale * inverse for scale in scales]
+    parts = []
+    for pair in range(heads // 2):
+        block = slice(pair * lanes, (pair + 1) * lanes)
+        total = None
+        for s in range(shards):
+            spread = jnp.where(
+                low,
+                jnp.broadcast_to(factors[s][:, 2 * pair : 2 * pair + 1], (batch, lanes)),
+                jnp.broadcast_to(factors[s][:, 2 * pair + 1 : 2 * pair + 2], (batch, lanes)),
+            )
+            term = spread * o_all[s, :, block].astype(jnp.float32)
+            total = term if total is None else total + term
+        att_ref[:, block] = total
+        parts.append(total.astype(jnp.bfloat16))
+    attended = jnp.concatenate(parts, axis=1)
+
+    p_all[my_tp] = jnp.dot(attended, wo_vm[...], preferred_element_type=jnp.float32)
+    p_copies = [
+        push(p_all.at[my_tp], p_all.at[my_tp], p_send.at[slot], p_recv.at[slot], {"tp": peer})
+        for slot, peer in tp_peers
+    ]
+    gate_row = jnp.sum(jnp.where(ids_ref[...] == mine, gp_ref[...], 0.0), axis=0, keepdims=True)
+    square = (batch, batch)
+    diagonal = lax.broadcasted_iota(jnp.int32, square, 0) == lax.broadcasted_iota(jnp.int32, square, 1)
+    expert_gate = jnp.sum(jnp.where(diagonal, jnp.broadcast_to(gate_row, square), 0.0), axis=1, keepdims=True)
+    for copy in p_copies:
+        copy.wait_recv()
+    projected = p_all[0]
+    for s in range(1, tps):
+        projected = projected + p_all[s]
+    hidden = (projected + res_ref[...].astype(jnp.float32)).astype(jnp.bfloat16)
+    h_all[mine] = hidden
+    h_copies = [
+        push(h_all.at[mine], h_all.at[mine], h_send.at[slot], h_recv.at[slot], {"kvp": peer})
+        for slot, peer in kvp_peers
+    ]
+    wg_load.wait()
+    wu_load.wait()
+    wd_load.wait()
+    for copy in g_copies:
+        copy.wait_recv()
+    for copy in h_copies:
+        copy.wait_recv()
+
+    states = [h_all[s].astype(jnp.float32) for s in range(shards)]
+    squares = None
+    for state in states:
+        term = state * state
+        squares = term if squares is None else squares + term
+    root = lax.rsqrt(jnp.sum(squares, axis=1, keepdims=True) / NORM_WIDTH + EPSILON)
+    normed = jnp.concatenate(
+        [(states[s] * root * gain_all[s, 0:1, :]).astype(jnp.bfloat16) for s in range(shards)], axis=1
+    )
+    gate_proj = jnp.dot(normed, wg_vm[0], preferred_element_type=jnp.float32)
+    up_proj = jnp.dot(normed, wu_vm[0], preferred_element_type=jnp.float32)
+    activation = (gate_proj / (1.0 + jnp.exp(-gate_proj)) * up_proj).astype(jnp.bfloat16)
+    expert_out = jnp.dot(activation, wd_vm[0], preferred_element_type=jnp.float32) * expert_gate
+    for s in range(shards):
+        y_send[s] = expert_out[:, s * cols : (s + 1) * cols].astype(y_send.dtype)
+    y_copies = [
+        push(y_send.at[peer], y_recv.at[mine], ys_send.at[slot], ys_recv.at[slot], {"kvp": peer})
+        for slot, peer in kvp_peers
+    ]
+    y_recv[mine] = y_send[mine]
+    for copy in y_copies:
+        copy.wait_recv()
+    term = y_recv[0].astype(jnp.float32)
+    for s in range(1, shards):
+        term = term + y_recv[s].astype(jnp.float32)
+    z_all[my_tp] = term.astype(z_all.dtype)
+    z_copies = [
+        push(z_all.at[my_tp], z_all.at[my_tp], z_send.at[slot], z_recv.at[slot], {"tp": peer})
+        for slot, peer in tp_peers
+    ]
+    for copy in z_copies:
+        copy.wait_recv()
+    moe = z_all[0].astype(jnp.float32)
+    for s in range(1, tps):
+        moe = moe + z_all[s].astype(jnp.float32)
+    mix_ref[...] = (hidden.astype(jnp.float32) + moe).astype(jnp.bfloat16)
+    for copy in sent:
+        copy.wait_send()
+
+
+def on_device_fused(
+    queries, keys, values, lengths, out_weight, residual, norm_gain, expert_ids, gate_probs, w_gate, w_up, w_down
+):
+    shards = lax.axis_size("kvp")
+    tps = lax.axis_size("tp")
+    batch, width = queries.shape
+    heads = width // HEAD
+    ctx, lanes = keys.shape[1:]
+    cols = residual.shape[1]
+    vmem = pl.BlockSpec(memory_space=pltpu.VMEM)
+    anywhere = pl.BlockSpec(memory_space=pltpu.HBM)
+    smem = pl.BlockSpec(memory_space=pltpu.SMEM)
+    f32, b16 = jnp.float32, jnp.bfloat16
+
+    def sems(count):
+        return pltpu.SemaphoreType.DMA((max(count, 1),))
+
+    k, t = shards - 1, tps - 1
+    return tuple(pl.pallas_call(
+        fused,
+        out_shape=(
+            jax.ShapeDtypeStruct((batch, width), f32),
+            jax.ShapeDtypeStruct((batch, cols), b16),
+        ),
+        in_specs=[anywhere, anywhere, anywhere, smem, anywhere, vmem, vmem, vmem, vmem, anywhere, anywhere, anywhere],
+        out_specs=(vmem, vmem),
+        scratch_shapes=[
+            pltpu.VMEM(queries.shape, b16),
+            pltpu.VMEM(keys.shape, b16),
+            pltpu.VMEM(values.shape, b16),
+            pltpu.VMEM(out_weight.shape, b16),
+            pltpu.VMEM(w_gate.shape, b16),
+            pltpu.VMEM(w_up.shape, b16),
+            pltpu.VMEM(w_down.shape, b16),
+            pltpu.VMEM((batch * heads, lanes), f32),
+            pltpu.VMEM((batch * heads, ctx), f32),
+            pltpu.VMEM((batch * heads, lanes), f32),
+            pltpu.VMEM((batch * heads, lanes), f32),
+            pltpu.VMEM((shards, batch, width), b16),
+            pltpu.VMEM((shards, batch, lanes), f32),
+            pltpu.VMEM((shards, 8, cols), f32),
+            pltpu.VMEM((tps, batch, cols), f32),
+            pltpu.VMEM((shards, batch, cols), b16),
+            pltpu.VMEM((shards, batch, cols), b16),
+            pltpu.VMEM((shards, batch, cols), b16),
+            pltpu.VMEM((tps, batch, cols), f32),
+            sems(7), sems(k), sems(k), sems(k), sems(k), sems(k), sems(k),
+            sems(t), sems(t), sems(k), sems(k), sems(k), sems(k), sems(t), sems(t),
+        ],
+        compiler_params=pltpu.CompilerParams(
+            collective_id=0, has_side_effects=True, vmem_limit_bytes=60 * 1024 * 1024
+        ),
+    )(
+        queries, keys, values, lengths, out_weight, residual, norm_gain,
+        expert_ids.T, gate_probs.T, w_gate, w_up, w_down,
+    ))
+
+
+def body(queries, keys, values, lengths, out_weight, residual, norm_gain, expert_ids, gate_probs, w_gate, w_up, w_down):
+    args = (queries, keys, values, lengths, out_weight, residual, norm_gain, expert_ids, gate_probs, w_gate, w_up, w_down)
+    fits = (
+        keys.shape[1] == 128
+        and keys.shape[2] == 2 * HEAD
+        and w_gate.shape[0] == 1
+        and residual.shape[1] % 128 == 0
+        and queries.shape[0] % 16 == 0
+        and (queries.shape[1] // HEAD) % 16 == 0
+    )
+    return on_device_fused(*args) if fits else on_device(*args)
+
+
 def solution(mesh):
     return jax.shard_map(
-        on_device,
+        body,
         mesh=mesh,
         in_specs=(
             P("grp", "tp"),

time: 126 us -> 30.2 us (0.24)
  blocking collectives: 93.8 us -> 0 us
  Pallas kernels: 0 us -> 26.5 us
  other arithmetic: 15.3 us -> 0 us
  matrix products: 6.53 us -> 0 us
  local copies, waits for them, and re-layouts: 8.31 us -> 2.78 us
    all_gather x3 -> x0, blocking collectives: 43.4 us -> none  [merged(): gathered = jax.tree.map(lambda a: lax.all_gather(a, axis), part)]
    psum x3 -> x0, blocking collectives: 34.1 us -> none  [the longest x1 12.5 us: on_device(): total_sq = lax.psum(jnp.sum(state_wide * state_wide, axis=1), 'kvp')]
    pallas_call x0 -> x1, Pallas kernels: none -> 26.5 us  [on_device_fused(): pl.pallas_call(fused, out_shape=(jax.ShapeDtypeStruct((batch, width), f32...]
    all_to_all x2 -> x0, blocking collectives: 16.3 us -> none  [the longest x1 8.21 us: on_device(): lax.all_to_all(partial_value, 'kvp', split_axis=2, concat_axis=0, tiled=T...]
    unnamed x1 -> x0, other arithmetic: 7.21 us -> none
    dot_general x7 -> x0, matrix products: 6.53 us -> none  [the longest x1 2.07 us: on_device(): jnp.dot(attended.astype(jnp.bfloat16), out_weight, preferred_element_type...]
    unnamed x19 -> x2, local copies, waits for them, and re-layouts: 5.3 us -> 2.78 us
    reduce_sum x4 -> x0, other arithmetic: 2.39 us -> none  [the longest x1 1.37 us: slot_tables(): dispatch = jnp.sum(hit_table, axis=1)]
where the time goes in v1:
time: 30.2 us; the launch traced here: 29.9 us
  Pallas kernels  26.5 us (88%)
  local copies, waits for them, and re-layouts  2.78 us (9%)
  between operations  0.64 us (2%)
    pallas_call x1, Pallas kernels, on_device_fused(): pl.pallas_call(fused, out_shape=(jax.ShapeDtypeStruct((batch, width), f32...  26.5 us
    unnamed x2, local copies, waits for them, and re-layouts  2.78 us

profile of v1, /device:TPU:0, one launch (start us, length us, event | category | flops | bytes accessed | tf_op | source)
XLA Modules:
  0.0 29.9 jit_solution(14900847312943676224)
XLA Ops:
  0.6 26.5 %shard_map.131 = (f32[16,1024]{1,0:T(8,128)}, bf16[16,384]{1,0:T(8,128)(2,1)}) custom-call(bf16[16,1024]{1,0:T(8,128)(2,1)} %q_hbm.1, bf16[16,128,128]{2,1,0:T(8,128)(2,1)} %k_hbm.1, bf16[16,128,128]{2,1,0:T(8,128)(2,1)} %v_hbm.1, s32[16]{0:T(128)} %len_ref.1, bf16[1024,384]{1,0:T(8,128)(2,1)} %wo_hbm.1, bf16[16,384]{1,0:T(8,128)(2,1)} %res_ref.1, ...), custom_call_target="tpu_custom_call" | custom-call | tf_op jit(solution)/shard_map/pallas_call | solution.py:367
  27.1 1.5 %copy.16 = f32[16,1024]{1,0:T(8,128)} copy(f32[16,1024]{1,0:T(8,128)} %get-tuple-element.4) | data formatting | bytes 131072
  28.6 1.3 %copy.17 = bf16[16,384]{1,0:T(8,128)(2,1)} copy(bf16[16,384]{1,0:T(8,128)(2,1)} %get-tuple-element.5) | data formatting | bytes 24576

commit v2 on v1

--- a/solution.py
+++ b/solution.py
@@ -142,9 +142,9 @@
 
 
 def fused(
-    q_hbm, k_hbm, v_hbm, len_ref, wo_hbm, res_ref, gain_ref, ids_ref, gp_ref, wg_hbm, wu_hbm, wd_hbm,
+    q_hbm, k_hbm, v_hbm, len_hbm, wo_hbm, res_hbm, gain_hbm, ids_hbm, gp_hbm, wg_hbm, wu_hbm, wd_hbm,
     att_ref, mix_ref,
-    q_vm, k_vm, v_vm, wo_vm, wg_vm, wu_vm, wd_vm,
+    q_vm, k_vm, v_vm, len_ref, wo_vm, res_ref, gain_ref, ids_ref, gp_ref, wg_vm, wu_vm, wd_vm,
     q_rows, s_rows, o_rows, t_rows,
     o_all, stat_all, gain_all, p_all, h_all, y_send, y_recv, z_all,
     load_sem, o_send, o_recv, st_send, st_recv, g_send, g_recv,
@@ -163,20 +163,29 @@
     kvp_peers = peers("kvp")
     tp_peers = peers("tp")
 
-    loads = []
-    for index, (source, target) in enumerate(
-        ((q_hbm, q_vm), (k_hbm, k_vm), (v_hbm, v_vm), (wo_hbm, wo_vm), (wg_hbm, wg_vm), (wu_hbm, wu_vm), (wd_hbm, wd_vm))
-    ):
-        copy = pltpu.make_async_copy(source, target, load_sem.at[index])
-        copy.start()
-        loads.append(copy)
-    q_load, k_load, v_load, wo_load, wg_load, wu_load, wd_load = loads
-
     barrier = pltpu.get_barrier_semaphore()
     for _, peer in kvp_peers:
         pl.semaphore_signal(barrier, inc=1, device_id={"kvp": peer}, device_id_type=MESH)
     for _, peer in tp_peers:
         pl.semaphore_signal(barrier, inc=1, device_id={"tp": peer}, device_id_type=MESH)
+
+    def load(index, source, target):
+        return pltpu.make_async_copy(source, target, load_sem.at[index])
+
+    len_load = load(0, len_hbm, len_ref)
+    q_load = load(1, q_hbm, q_vm)
+    k_load = load(2, k_hbm, k_vm)
+    v_load = load(3, v_hbm, v_vm)
+    res_load = load(4, res_hbm, res_ref)
+    gain_load = load(5, gain_hbm, gain_ref)
+    ids_load = load(6, ids_hbm, ids_ref)
+    gp_load = load(7, gp_hbm, gp_ref)
+    wo_load = load(8, wo_hbm, wo_vm)
+    wg_load = load(9, wg_hbm, wg_vm)
+    wu_load = load(10, wu_hbm, wu_vm)
+    wd_load = load(11, wd_hbm, wd_vm)
+    for copy in (q_load, len_load, k_load, v_load, gain_load, res_load, ids_load, gp_load):
+        copy.start()
 
     sent = []
 
@@ -191,7 +200,6 @@
 
     lane = lax.broadcasted_iota(jnp.int32, (batch, lanes), 1)
     low = lane < HEAD
-    gain_all[mine] = jnp.broadcast_to(gain_ref[...].astype(jnp.float32).reshape(1, cols), (8, cols))
 
     q_load.wait()
     for head in range(heads):
@@ -202,7 +210,9 @@
             kept = pltpu.roll(kept, HEAD, 1)
         q_rows[pl.ds(head, batch, stride=heads), :] = kept
 
+    len_load.wait()
     k_load.wait()
+    wo_load.start()
     position = mine * ctx + lax.broadcasted_iota(jnp.int32, (heads, ctx), 1)
     for b in range(batch):
         rows = pl.ds(b * heads, heads)
@@ -212,6 +222,9 @@
         ) * HEAD ** (-0.5)
         s_rows[rows, :] = jnp.where(position < len_ref[b], scores, NEGATIVE)
     v_load.wait()
+    wg_load.start()
+    wu_load.start()
+    wd_load.start()
     stat_low = lax.broadcasted_iota(jnp.int32, (heads, lanes), 1) < HEAD
     for b in range(batch):
         rows = pl.ds(b * heads, heads)
@@ -236,6 +249,8 @@
         stat = jnp.where((lane == head) | (lane == HEAD + head), t_rows[head * batch : (head + 1) * batch, :], stat)
     stat_all[mine] = stat
 
+    gain_load.wait()
+    gain_all[mine] = jnp.broadcast_to(gain_ref[...].astype(jnp.float32).reshape(1, cols), (8, cols))
     pl.semaphore_wait(barrier, len(kvp_peers) + len(tp_peers))
     o_copies = []
     for slot, peer in kvp_peers:
@@ -245,7 +260,8 @@
         push(gain_all.at[mine], gain_all.at[mine], g_send.at[slot], g_recv.at[slot], {"kvp": peer})
         for slot, peer in kvp_peers
     ]
-    wo_load.wait()
+    for copy in (wo_load, res_load, ids_load, gp_load):
+        copy.wait()
     for copy in o_copies:
         copy.wait_recv()
 
@@ -356,8 +372,7 @@
     ctx, lanes = keys.shape[1:]
     cols = residual.shape[1]
     vmem = pl.BlockSpec(memory_space=pltpu.VMEM)
-    anywhere = pl.BlockSpec(memory_space=pltpu.HBM)
-    smem = pl.BlockSpec(memory_space=pltpu.SMEM)
+    anywhere = pl.BlockSpec(memory_space=pl.ANY)
     f32, b16 = jnp.float32, jnp.bfloat16
 
     def sems(count):
@@ -367,16 +382,21 @@
     return tuple(pl.pallas_call(
         fused,
         out_shape=(
-            jax.ShapeDtypeStruct((batch, width), f32),
-            jax.ShapeDtypeStruct((batch, cols), b16),
+            pltpu.VMEM((batch, width), f32),
+            pltpu.VMEM((batch, cols), b16),
         ),
-        in_specs=[anywhere, anywhere, anywhere, smem, anywhere, vmem, vmem, vmem, vmem, anywhere, anywhere, anywhere],
+        in_specs=[anywhere] * 12,
         out_specs=(vmem, vmem),
         scratch_shapes=[
             pltpu.VMEM(queries.shape, b16),
             pltpu.VMEM(keys.shape, b16),
             pltpu.VMEM(values.shape, b16),
+            pltpu.SMEM(lengths.shape, jnp.int32),
             pltpu.VMEM(out_weight.shape, b16),
+            pltpu.VMEM(residual.shape, b16),
+            pltpu.VMEM(norm_gain.shape, b16),
+            pltpu.VMEM(expert_ids.shape[::-1], jnp.int32),
+            pltpu.VMEM(gate_probs.shape[::-1], f32),
             pltpu.VMEM(w_gate.shape, b16),
             pltpu.VMEM(w_up.shape, b16),
             pltpu.VMEM(w_down.shape, b16),
@@ -392,7 +412,7 @@
             pltpu.VMEM((shards, batch, cols), b16),
             pltpu.VMEM((shards, batch, cols), b16),
             pltpu.VMEM((tps, batch, cols), f32),
-            sems(7), sems(k), sems(k), sems(k), sems(k), sems(k), sems(k),
+            sems(12), sems(k), sems(k), sems(k), sems(k), sems(k), sems(k),
             sems(t), sems(t), sems(k), sems(k), sems(k), sems(k), sems(t), sems(t),
         ],
         compiler_params=pltpu.CompilerParams(

time: 30.2 us -> 27.2 us (0.901)
  local copies, waits for them, and re-layouts: 2.78 us -> 1.23 us
  Pallas kernels: 26.5 us -> 25.2 us
    unnamed x2, local copies, waits for them, and re-layouts: 2.78 us -> 1.23 us
    pallas_call x1, Pallas kernels: 26.5 us -> 25.2 us  [on_device_fused(): pl.pallas_call(fused, out_shape=(pltpu.VMEM((batch, width), f32), pltpu.V...]
where the time goes in v2:
time: 27.2 us; the launch traced here: 27.1 us
  Pallas kernels  25.2 us (93%)
  local copies, waits for them, and re-layouts  1.23 us (5%)
  between operations  0.64 us (2%)
    pallas_call x1, Pallas kernels, on_device_fused(): pl.pallas_call(fused, out_shape=(pltpu.VMEM((batch, width), f32), pltpu.V...  25.2 us
    unnamed x2, local copies, waits for them, and re-layouts  1.23 us

profile of v2, /device:TPU:0, one launch (start us, length us, event | category | flops | bytes accessed | tf_op | source)
XLA Modules:
  0.0 27.1 jit_solution(17601900675711036937)
XLA Ops:
  0.6 25.2 %shard_map.131 = (f32[16,1024]{1,0:T(8,128)S(1)}, bf16[16,384]{1,0:T(8,128)(2,1)S(1)}) custom-call(bf16[16,1024]{1,0:T(8,128)(2,1)} %q_hbm.1, bf16[16,128,128]{2,1,0:T(8,128)(2,1)} %k_hbm.1, bf16[16,128,128]{2,1,0:T(8,128)(2,1)} %v_hbm.1, s32[16]{0:T(128)} %len_hbm.1, bf16[1024,384]{1,0:T(8,128)(2,1)} %wo_hbm.1, bf16[16,384]{1,0:T(8,128)(2,1)} %res_hbm.1, ...), custom_call_target="tpu_custom_call" | custom-call | tf_op jit(solution)/shard_map/pallas_call | solution.py:382
  25.8 0.6 %copy.16 = f32[16,1024]{1,0:T(8,128)} copy(f32[16,1024]{1,0:T(8,128)S(1)} %get-tuple-element.2) | data formatting | bytes 131072
  26.5 0.6 %copy.17 = bf16[16,384]{1,0:T(8,128)(2,1)} copy(bf16[16,384]{1,0:T(8,128)(2,1)S(1)} %get-tuple-element.3) | data formatting | bytes 24576

commit v3 on v2

--- a/solution.py
+++ b/solution.py
@@ -1,3 +1,5 @@
+import functools
+
 import jax
 import jax.numpy as jnp
 from jax import lax
@@ -247,31 +249,30 @@
         o_all[mine, :, pair * lanes : (pair + 1) * lanes] = jnp.where(low, first, second).astype(jnp.bfloat16)
     for head in range(heads):
         stat = jnp.where((lane == head) | (lane == HEAD + head), t_rows[head * batch : (head + 1) * batch, :], stat)
-    stat_all[mine] = stat
+    half = batch // 2
+    fold = lax.rem(lane[:half], HEAD) < heads
+    stat_all[mine] = jnp.where(fold, stat[:half], pltpu.roll(stat[half:], heads, 1))
 
     gain_load.wait()
-    gain_all[mine] = jnp.broadcast_to(gain_ref[...].astype(jnp.float32).reshape(1, cols), (8, cols))
+    gain_all[mine] = jnp.broadcast_to(gain_ref[...].astype(jnp.float32).reshape(1, cols), (1, cols))
     pl.semaphore_wait(barrier, len(kvp_peers) + len(tp_peers))
     o_copies = []
     for slot, peer in kvp_peers:
         o_copies.append(push(stat_all.at[mine], stat_all.at[mine], st_send.at[slot], st_recv.at[slot], {"kvp": peer}))
         o_copies.append(push(o_all.at[mine], o_all.at[mine], o_send.at[slot], o_recv.at[slot], {"kvp": peer}))
-    g_copies = [
-        push(gain_all.at[mine], gain_all.at[mine], g_send.at[slot], g_recv.at[slot], {"kvp": peer})
-        for slot, peer in kvp_peers
-    ]
     for copy in (wo_load, res_load, ids_load, gp_load):
         copy.wait()
     for copy in o_copies:
         copy.wait_recv()
 
-    global_max = stat_all[0]
-    for s in range(1, shards):
-        global_max = jnp.maximum(global_max, stat_all[s])
+    stats = [
+        jnp.concatenate([stat_all[s], pltpu.roll(stat_all[s], lanes - heads, 1)], axis=0) for s in range(shards)
+    ]
+    global_max = functools.reduce(jnp.maximum, stats)
     scales = []
     denominator = None
     for s in range(shards):
-        stat = stat_all[s]
+        stat = stats[s]
         scale = jnp.exp(stat - global_max)
         scales.append(scale)
         term = scale * pltpu.roll(stat, HEAD, 1)
@@ -298,6 +299,10 @@
     p_copies = [
         push(p_all.at[my_tp], p_all.at[my_tp], p_send.at[slot], p_recv.at[slot], {"tp": peer})
         for slot, peer in tp_peers
+    ]
+    g_copies = [
+        push(gain_all.at[mine], gain_all.at[mine], g_send.at[slot], g_recv.at[slot], {"kvp": peer})
+        for slot, peer in kvp_peers
     ]
     gate_row = jnp.sum(jnp.where(ids_ref[...] == mine, gp_ref[...], 0.0), axis=0, keepdims=True)
     square = (batch, batch)
@@ -405,8 +410,8 @@
             pltpu.VMEM((batch * heads, lanes), f32),
             pltpu.VMEM((batch * heads, lanes), f32),
             pltpu.VMEM((shards, batch, width), b16),
-            pltpu.VMEM((shards, batch, lanes), f32),
-            pltpu.VMEM((shards, 8, cols), f32),
+            pltpu.VMEM((shards, batch // 2, lanes), f32),
+            pltpu.VMEM((shards, 1, cols), f32),
             pltpu.VMEM((tps, batch, cols), f32),
             pltpu.VMEM((shards, batch, cols), b16),
             pltpu.VMEM((shards, batch, cols), b16),
@@ -431,8 +436,8 @@
         and keys.shape[2] == 2 * HEAD
         and w_gate.shape[0] == 1
         and residual.shape[1] % 128 == 0
-        and queries.shape[0] % 16 == 0
-        and (queries.shape[1] // HEAD) % 16 == 0
+        and queries.shape[0] == 16
+        and queries.shape[1] // HEAD == 16
     )
     return on_device_fused(*args) if fits else on_device(*args)
 

time: 27.2 us -> 26.4 us (0.971)
  Pallas kernels: 25.2 us -> 24.3 us
    pallas_call x1, Pallas kernels: 25.2 us -> 24.3 us  [on_device_fused(): pl.pallas_call(fused, out_shape=(pltpu.VMEM((batch, width), f32), pltpu.V...]
where the time goes in v3:
time: 26.4 us; the launch traced here: 26.2 us
  Pallas kernels  24.3 us (92%)
  local copies, waits for them, and re-layouts  1.23 us (5%)
  between operations  0.64 us (2%)
    pallas_call x1, Pallas kernels, on_device_fused(): pl.pallas_call(fused, out_shape=(pltpu.VMEM((batch, width), f32), pltpu.V...  24.3 us
    unnamed x2, local copies, waits for them, and re-layouts  1.23 us

profile of v3, /device:TPU:0, one launch (start us, length us, event | category | flops | bytes accessed | tf_op | source)
XLA Modules:
  0.0 26.2 jit_solution(14560826761023981507)
XLA Ops:
  0.6 24.3 %shard_map.131 = (f32[16,1024]{1,0:T(8,128)S(1)}, bf16[16,384]{1,0:T(8,128)(2,1)S(1)}) custom-call(bf16[16,1024]{1,0:T(8,128)(2,1)} %q_hbm.1, bf16[16,128,128]{2,1,0:T(8,128)(2,1)} %k_hbm.1, bf16[16,128,128]{2,1,0:T(8,128)(2,1)} %v_hbm.1, s32[16]{0:T(128)} %len_hbm.1, bf16[1024,384]{1,0:T(8,128)(2,1)} %wo_hbm.1, bf16[16,384]{1,0:T(8,128)(2,1)} %res_hbm.1, ...), custom_call_target="tpu_custom_call" | custom-call | tf_op jit(solution)/shard_map/pallas_call | solution.py:387
  25.0 0.6 %copy.16 = f32[16,1024]{1,0:T(8,128)} copy(f32[16,1024]{1,0:T(8,128)S(1)} %get-tuple-element.2) | data formatting | bytes 131072
  25.6 0.6 %copy.17 = bf16[16,384]{1,0:T(8,128)(2,1)} copy(bf16[16,384]{1,0:T(8,128)(2,1)S(1)} %get-tuple-element.3) | data formatting | bytes 24576
